TPU v7x, 32 devices: a whole 2x2x4 slice. The times are simulated.
32 devices in a mesh: groups: 2 (over y), expert: 4 (over z), tensor: 4 (over x, core).
Axes of the slice: x: 2, y: 2, z: 4, core: 2. Of those that a mesh axis runs over, the one named last changes fastest.
Arguments:
- tokens: bfloat16 [1024, 4096], P(('groups', 'expert'), 'tensor'), parts along dimension 0, may hold values from -6 to 6
- expert_ids: int32 [1024, 2], P(('groups', 'expert')), parts along dimension 0, may hold values from 0 to 31, all different within a row; in each aligned block of 128 rows (0 to 127, 128 to 255, ...) at most 16 rows name the same one
- gate_values: float32 [1024, 2], P(('groups', 'expert')), parts along dimension 0, may hold values from 0.3 to 1
- teacher_out: float32 [1024, 4096], P(('groups', 'expert'), 'tensor'), parts along dimension 0, may hold values from -6 to 6
- student_gate: bfloat16 [64, 512, 4096], P('expert', 'tensor'), may hold values from -0.09375 to 0.09375
- student_up: bfloat16 [64, 512, 4096], P('expert', 'tensor'), may hold values from -0.09375 to 0.09375
- student_down: bfloat16 [64, 512, 4096], P('expert', None, 'tensor'), may hold values from -0.1875 to 0.1875
Outputs:
- student: float32 [1024, 4096], P(('groups', 'expert'), 'tensor'), parts along dimension 0
- residual: float32 [1024, 4096], P(('groups', 'expert'), 'tensor'), parts along dimension 0
There are 2 independent parts, one for each index of `groups`. A program takes and returns all parts, laid end to end along the dimension named above; an argument that names none is the same for every part. Nothing has to cross between parts.
Inputs may be any that keep to these rules, and one draw needn't show every extreme that they name: `expert_ids`: each row names 2 different experts. In each aligned block of 128 rows (the rows of one index of expert) no expert is named by more than 16 rows, a bound that some block reaches.
All inputs are finite; a program needn't handle non-finite values.
Results may differ from a plain program's by a relative error of at most 0.0029.
Values may be sent and summed in bfloat16 or wider, within the bound.
A program may use at most 128 MiB of HBM per device.

v0:
```python
import jax
import jax.numpy as jnp
from jax import lax
from jax.sharding import PartitionSpec as P

EXPERTS = 32
TOP = 2
CAP = 16


def per_device(
    tokens, expert_ids, gate_values, teacher_out, student_gate, student_up, student_down
):
    row_count = tokens.shape[0]
    flat_ids = expert_ids.reshape(-1)
    onehot = (flat_ids[:, None] == jnp.arange(EXPERTS, dtype=jnp.int32)[None, :]).astype(jnp.int32)
    earlier = jnp.cumsum(onehot, axis=0) - onehot
    position = jnp.sum(earlier * onehot, axis=1)
    slot_ids = flat_ids * CAP + position
    slot_match = slot_ids[None, :] == jnp.arange(EXPERTS * CAP, dtype=jnp.int32)[:, None]
    picker = jnp.sum(
        slot_match.reshape(EXPERTS * CAP, row_count, TOP).astype(jnp.float32), axis=2
    ).astype(jnp.bfloat16)
    flat_gates = gate_values.reshape(-1)
    weighted = jnp.where(slot_match, flat_gates[None, :], jnp.zeros_like(flat_gates)[None, :])
    combiner = jnp.sum(weighted.reshape(EXPERTS * CAP, row_count, TOP), axis=2)
    width = tokens.shape[1]
    packed = jnp.dot(picker, tokens, preferred_element_type=jnp.float32).astype(jnp.bfloat16)
    doubled = jnp.broadcast_to(packed.reshape(EXPERTS, 1, CAP, width), (EXPERTS, 2, CAP, width))
    full_rows = lax.all_gather(
        lax.all_to_all(
            doubled.reshape(2 * EXPERTS, CAP, width),
            "expert",
            split_axis=0,
            concat_axis=0,
            tiled=True,
        ),
        "tensor",
        axis=2,
        tiled=True,
    )
    slab_local = student_gate.shape[0]
    source_count = full_rows.shape[0] // slab_local
    slot_count = full_rows.shape[1]
    grouped = full_rows.reshape(source_count, slab_local, slot_count, full_rows.shape[2])
    gate_pre = jnp.einsum(
        "nsid,shd->nsih", grouped, student_gate, preferred_element_type=jnp.float32
    )
    up_pre = jnp.einsum("nsid,shd->nsih", grouped, student_up, preferred_element_type=jnp.float32)
    activated = (jax.nn.silu(gate_pre) * up_pre).astype(jnp.bfloat16)
    whole_hidden = lax.all_gather(activated, "tensor", axis=3, tiled=True)
    outputs = jnp.einsum(
        "nsih,shd->nsid", whole_hidden, student_down, preferred_element_type=jnp.float32
    )
    flat_out = outputs.reshape(source_count * slab_local, slot_count, outputs.shape[3])
    returned_sum = lax.all_to_all(flat_out, "expert", split_axis=0, concat_axis=0, tiled=True)
    quarter_width = returned_sum.shape[2]
    halves_added = jnp.sum(returned_sum.reshape(EXPERTS, 2, CAP, quarter_width), axis=1).reshape(
        EXPERTS * CAP, quarter_width
    )
    student = lax.dot_general(
        combiner,
        halves_added,
        (((0,), (0,)), ((), ())),
        precision=lax.Precision.HIGHEST,
        preferred_element_type=jnp.float32,
    )
    return (student, teacher_out - student)


def solution(mesh):
    in_specs = (
        P(("groups", "expert"), "tensor"),
        P(("groups", "expert"), None),
        P(("groups", "expert"), None),
        P(("groups", "expert"), "tensor"),
        P("expert", "tensor", None),
        P("expert", "tensor", None),
        P("expert", None, "tensor"),
    )
    out_specs = (P(("groups", "expert"), "tensor"), P(("groups", "expert"), "tensor"))
    return jax.shard_map(
        per_device, mesh=mesh, in_specs=in_specs, out_specs=out_specs, check_vma=False
    )
```

profile of v0, /device:TPU:0, one launch (start us, length us, event | category | flops | bytes accessed | tf_op | source)
XLA Modules:
  0.0 279.9 jit_solution(94254755609666961)
XLA Ops:
  7.2 0.0 copy-start
  7.2 0.0 all-gather.3.cloned.1.call-start
  7.2 0.8 copy.28
  8.0 0.1 eq.44
  8.2 0.1 eq.40
  8.3 0.6 reduce-window.6
  8.9 0.2 slice_reduce_fusion
  9.2 0.1 fusion.34
  9.3 0.1 reduce_sum.39
  9.4 0.1 copy.31
  9.5 0.7 multiply_add_fusion
  10.2 0.8 convert_reduce_fusion
  11.0 0.0 copy-done
  11.0 0.4 convolution_convert_fusion
  11.4 0.3 broadcast_in_dim.29
  11.7 54.4 %all_to_all.10 = bf16[64,16,1024]{2,1,0:T(8,128)(2,1)} all-to-all(bf16[64,16,1024]{2,1,0:T(8,128)(2,1)S(1)} %bitcast.70), channel_id=1, replica_groups=mesh['groups'=2,'expert'=4,'tensor'=4] {'expert'}, dimensions={0} | all-to-all | bytes 4194304 | tf_op jit(solution)/shard_map/all_to_all | solution.py:31
  66.1 0.0 all-gather.3.cloned.1.call-update
  66.2 0.0 all-gather.5.cloned.1.call-start
  66.2 57.6 %all-gather.3.cloned.1.call-done = bf16[64,16,4096]{2,1,0:T(8,128)(2,1)} async-done(((bf16[64,16,1024]{2,1,0:T(8,128)(2,1)}), bf16[64,16,4096]{2,1,0:T(8,128)(2,1)}) %all-gather.3.cloned.1.call-update) | async-done | bytes 8388624 | tf_op jit(solution)/shard_map/all_gather | solution.py:30
  123.8 0.0 copy-start.2
  123.8 11.4 %fusion.11 = f32[4,16,16,128]{3,2,0,1:T(8,128)S(1)} fusion(bf16[16,128,4096]{2,1,0:T(8,128)(2,1)} %param.11, bf16[4,16,16,4096]{3,2,1,0:T(8,128)(2,1)} %bitcast.67), kind=kOutput, calls=%fused_computation.11 | convolution fusion | flops 1073741824 | bytes 25690112 | tf_op jit(solution)/shard_map/nsid,shd->nsih/dot_general | solution.py:46
  135.2 0.0 copy-done.2
  135.2 10.3 %fusion.26 = bf16[4,16,16,128]{3,2,0,1:T(8,128)(2,1)} fusion(bf16[16,128,4096]{2,1,0:T(8,128)(2,1)} %param.12, bf16[4,16,16,4096]{3,2,1,0:T(8,128)(2,1)S(1)} %bitcast.68, f32[4,16,16,128]{3,2,0,1:T(8,128)S(1)} %fusion.11), kind=kOutput, calls=%fused_computation.14 | convolution fusion | flops 1074528256 | bytes 25952256 | tf_op jit(solution)/shard_map/nsid,shd->nsih/dot_general | solution.py:49
  145.5 0.0 all-gather.5.cloned.1.call-update
  145.5 17.0 %all-gather.5.cloned.1.call-done = bf16[4,16,16,512]{3,2,0,1:T(8,128)(2,1)} async-done(((bf16[4,16,16,128]{3,2,0,1:T(8,128)(2,1)}), bf16[4,16,16,512]{3,2,0,1:T(8,128)(2,1)}) %all-gather.5.cloned.1.call-update) | async-done | bytes 1048592 | tf_op jit(solution)/shard_map/all_gather | solution.py:51
  162.5 9.1 %fusion.8 = f32[4,16,16,1024]{3,2,0,1:T(8,128)S(1)} fusion(bf16[4,16,16,512]{3,2,0,1:T(8,128)(2,1)} %all-gather.5.cloned.1.call-done, bf16[16,512,1024]{2,1,0:T(8,128)(2,1)} %param.13), kind=kOutput, calls=%fused_computation.9 | convolution fusion | flops 1073741824 | bytes 22020096 | tf_op jit(solution)/shard_map/nsih,shd->nsid/dot_general | solution.py:52
  171.7 0.5 copy.34
  172.2 0.0 copy-start.3
  172.2 0.0 copy-start.1
  172.2 98.1 %all_to_all.11 = f32[64,16,1024]{2,1,0:T(8,128)S(1)} all-to-all(f32[64,16,1024]{2,1,0:T(8,128)S(1)} %bitcast.66), channel_id=1, replica_groups=mesh['groups'=2,'expert'=4,'tensor'=4] {'expert'}, dimensions={0} | all-to-all | bytes 8388608 | tf_op jit(solution)/shard_map/all_to_all | solution.py:56
  270.3 0.5 bitcast_reduce_fusion
  270.8 0.0 copy-done.3
  270.8 2.3 fusion.36
  273.1 0.0 copy-done.1
  (3 shorter events, 0.0 us)
Async XLA Ops:
  7.2 3.8 %copy-start = (bf16[128,1024]{1,0:T(8,128)(2,1)S(1)}, bf16[128,1024]{1,0:T(8,128)(2,1)}, u32[]{:S(2)}) copy-start(bf16[128,1024]{1,0:T(8,128)(2,1)} %param.7) | copy-start | bytes 786436
  7.2 116.6 %all-gather.3.cloned.1.call-start = ((), (), s32[]{:S(2)}) async-start(), calls=%async_computation.2 | async-start | bytes 10485760 | tf_op jit(solution)/shard_map/all_gather | solution.py:30
  66.2 96.4 %all-gather.5.cloned.1.call-start = ((), (), s32[]{:S(2)}) async-start(), calls=%async_computation.3 | async-start | bytes 1310720 | tf_op jit(solution)/shard_map/all_gather | solution.py:51
  123.8 11.4 %copy-start.2 = (bf16[64,16,4096]{2,1,0:T(8,128)(2,1)S(1)}, bf16[64,16,4096]{2,1,0:T(8,128)(2,1)}, u32[]{:S(2)}) copy-start(bf16[64,16,4096]{2,1,0:T(8,128)(2,1)} %all-gather.3.cloned.1.call-done) | copy-start | bytes 25165828
  172.2 98.6 %copy-start.3 = (f32[128,1024]{1,0:T(8,128)S(1)}, f32[128,1024]{1,0:T(8,128)}, u32[]{:S(2)}) copy-start(f32[128,1024]{1,0:T(8,128)} %param.10) | copy-start | bytes 1572868
  172.2 100.9 %copy-start.1 = (bf16[128,1024]{1,0:T(8,128)(2,1)S(1)}, bf16[128,1024]{1,0:T(8,128)(2,1)}, u32[]{:S(2)}) copy-start(bf16[128,1024]{1,0:T(8,128)(2,1)} %param.7) | copy-start | bytes 786436
Sparse Core Ops, SparseCore 0:
  66.3 57.4 all-gather.2
  145.6 16.8 all-gather.4
where the time goes:
time: 280 us
  blocking collectives  152 us (54%)
  waiting for transfers between devices  74.7 us (27%)
  matrix products  33.5 us (12%)
  between operations  14.2 us (5%)
    all_to_all x1, blocking collectives, per_device(): lax.all_to_all(flat_out, 'expert', split_axis=0, concat_axis=0, tiled=True)  98.1 us
    all_gather x1, waiting for transfers between devices, per_device(): lax.all_gather(lax.all_to_all(doubled.reshape(2 * EXPERTS, CAP, width), '...  57.6 us
    all_to_all x1, blocking collectives, per_device(): lax.all_to_all(doubled.reshape(2 * EXPERTS, CAP, width), 'expert', split_...  54.4 us
    all_gather x1, waiting for transfers between devices, per_device(): whole_hidden = lax.all_gather(activated, 'tensor', axis=3, tiled=True)  17 us
    dot_general x1, matrix products, per_device(): jnp.einsum('nsid,shd->nsih', grouped, student_gate, preferred_element_typ...  11.4 us
    dot_general x1, matrix products, per_device(): jnp.einsum('nsid,shd->nsih', grouped, student_up, preferred_element_type=...  10.3 us
    dot_general x1, matrix products, per_device(): jnp.einsum('nsih,shd->nsid', whole_hidden, student_down, preferred_elemen...  9.12 us
  transfers between devices with their start and end apart: 2, of which 2 were waited for; matrix products, arithmetic and copies ran while one was open for 0% of the time, Pallas kernels for 0%

commit v1 on v0

--- a/solution.py
+++ b/solution.py
@@ -1,6 +1,9 @@
+import functools
 import jax
 import jax.numpy as jnp
 from jax import lax
+from jax.experimental import pallas as pl
+from jax.experimental.pallas import tpu as pltpu
 from jax.sharding import PartitionSpec as P
 
 EXPERTS = 32
@@ -68,6 +71,305 @@
     return (student, teacher_out - student)
 
 
+def fused_kernel(
+    n, lead, lag, meta_ref, tok_ref, wg_ref, wu_ref, wd_ref, out_ref,
+    wgu, wdb, gath, sids, packed, acc, hid, outs, back,
+    wsem, dsem, zsend, zrecv, msend, mrecv, ssend, srecv, xsend, xrecv, fsend, frecv,
+    hsend, hrecv, rsend, rrecv,
+):
+    z, t = lax.axis_index("expert"), lax.axis_index("tensor")
+    sib = t + 1 - 2 * lax.rem(t, 2)
+    across = lax.rem(t + 2, 4)
+    order = (t, sib, across, lax.rem(sib + 2, 4))
+    rows, kd = tok_ref.shape
+    local, part = wg_ref.shape[0], wg_ref.shape[1]
+    half = part // 2
+    slots = local * CAP
+    f32, bf16 = jnp.float32, jnp.bfloat16
+
+    def remote(src, dst, send, recv, where):
+        return pltpu.make_async_remote_copy(
+            src_ref=src, dst_ref=dst, send_sem=send, recv_sem=recv,
+            device_id=where, device_id_type=pl.DeviceIdType.MESH,
+        )
+
+    weight_copies = []
+    for j in range(4):
+        cols = pl.ds(pl.multiple_of(order[j] * kd, kd), kd)
+        weight_copies.append((
+            pltpu.make_async_copy(wg_ref.at[:, :, cols], wgu.at[j, :, 0:part, :], wsem.at[j, 0]),
+            pltpu.make_async_copy(wu_ref.at[:, :, cols], wgu.at[j, :, part:2 * part, :], wsem.at[j, 1]),
+        ))
+    down_copies = []
+    for j in range(4):
+        for h in range(2):
+            hrows = pl.ds(pl.multiple_of(order[j] * half, half), half)
+            down_copies.append(pltpu.make_async_copy(
+                wd_ref.at[:, h, hrows, :],
+                wdb.at[:, pl.ds(j * part + h * half, half), :],
+                dsem.at[j, h],
+            ))
+    for pair in weight_copies:
+        for c in pair:
+            c.start()
+    for c in down_copies:
+        c.start()
+
+    barrier = pltpu.get_barrier_semaphore()
+    peers = [{"expert": lax.rem(z + i, n)} for i in range(1, n)]
+    peers += [{"tensor": order[j]} for j in range(1, 4)]
+    for peer in peers:
+        pl.semaphore_signal(barrier, inc=1, device_id=peer, device_id_type=pl.DeviceIdType.MESH)
+    pl.semaphore_wait(barrier, len(peers))
+
+    def tok_copy(d, src, own):
+        ref = tok_ref if own else gath.at[src]
+        return remote(ref, gath.at[src], zsend.at[d, src], zrecv.at[src], {"expert": z + 1 - 2 * d})
+
+    def sid_copy(d, src):
+        return remote(sids.at[src], sids.at[src], msend.at[d, src], mrecv.at[src], {"expert": z + 1 - 2 * d})
+
+    def each_way(fn):
+        @pl.when(z < n - 1)
+        def _():
+            fn(0)
+
+        @pl.when(z > 0)
+        def _():
+            fn(1)
+
+    each_way(lambda d: tok_copy(d, z, True).start())
+
+    id0, id1 = meta_ref[0:1, :], meta_ref[1:2, :]
+    names = lax.broadcasted_iota(jnp.int32, (n * local, rows), 0).astype(f32)
+    hit0, hit1 = names == id0, names == id1
+    hits = (jnp.where(hit0, 1.0, 0.0) + jnp.where(hit1, 1.0, 0.0)).astype(bf16)
+    before = jnp.where(
+        lax.broadcasted_iota(jnp.int32, (rows, rows), 0) < lax.broadcasted_iota(jnp.int32, (rows, rows), 1),
+        1.0, 0.0,
+    ).astype(bf16)
+    earlier = jnp.dot(hits, before, preferred_element_type=f32)
+    sid0 = id0 * CAP + jnp.sum(jnp.where(hit0, earlier, 0.0), axis=0, keepdims=True)
+    sid1 = id1 * CAP + jnp.sum(jnp.where(hit1, earlier, 0.0), axis=0, keepdims=True)
+    line = lax.broadcasted_iota(jnp.int32, (8, rows), 0)
+    sids[z] = jnp.where(line == 0, sid0, jnp.where(line == 1, sid1, 0.0))
+    each_way(lambda d: sid_copy(d, z).start())
+
+    slot_names = lax.broadcasted_iota(jnp.int32, (slots, rows), 0)
+
+    def sib_copy(src):
+        return remote(packed.at[0, src], packed.at[1, src], ssend.at[src], srecv.at[src], {"tensor": sib})
+
+    def across_copy(src):
+        return remote(packed.at[0, src], packed.at[2, src], xsend.at[src], xrecv.at[src], {"tensor": across})
+
+    def onward_copy(src):
+        return remote(packed.at[2, src], packed.at[3, src], fsend.at[src], frecv.at[src], {"tensor": sib})
+
+    def pick(src, own):
+        mine = (slot_names + z * slots).astype(f32)
+        a, b = sids[src, 0:1, :], sids[src, 1:2, :]
+        picker = (jnp.where(mine == a, 1.0, 0.0) + jnp.where(mine == b, 1.0, 0.0)).astype(bf16)
+        toks = tok_ref[...] if own else gath[src]
+        got = jnp.dot(picker, toks, preferred_element_type=f32).astype(bf16)
+        packed[0, src] = got.reshape(local, CAP, kd)
+        across_copy(src).start()
+        sib_copy(src).start()
+
+    def at_step(k, fn):
+        if k == 0:
+            fn(z, None)
+            return
+
+        @pl.when(z >= k)
+        def _():
+            fn(z - k, 0)
+
+        @pl.when(z + k < n)
+        def _():
+            fn(z + k, 1)
+
+    def can_forward(d):
+        return z < n - 1 if d == 0 else z > 0
+
+    def arrive(src, d):
+        tok_copy(d, src, False).wait_recv()
+        sid_copy(d, src).wait_recv()
+
+        @pl.when(can_forward(d))
+        def _():
+            tok_copy(d, src, False).start()
+            sid_copy(d, src).start()
+
+        pick(src, False)
+
+    def onward(src, d):
+        across_copy(src).wait_recv()
+        onward_copy(src).start()
+
+    pick(z, True)
+    for k in range(1, n):
+        at_step(k, arrive)
+        if k >= 2:
+            at_step(k - 2, onward)
+
+    nt = (((1,), (1,)), ((), ()))
+
+    def rows_of(j, e):
+        return packed[j, :, e].reshape(n * CAP, kd)
+
+    def partial(j, e):
+        return lax.dot_general(rows_of(j, e), wgu[j, e], nt, preferred_element_type=f32)
+
+    for s in range(n):
+        sib_copy(s).wait_recv()
+    for j in range(2):
+        for c in weight_copies[j]:
+            c.wait()
+
+    def first(e, carry):
+        acc[e] = partial(0, e) + partial(1, e)
+        return carry
+
+    lax.fori_loop(0, local, first, 0)
+
+    for k in range(max(n - 2, 0), n):
+        at_step(k, onward)
+    for s in range(n):
+        onward_copy(s).wait_recv()
+    for j in range(2, 4):
+        for c in weight_copies[j]:
+            c.wait()
+    for c in down_copies:
+        c.wait()
+
+    def hid_sib(e):
+        return remote(hid.at[e, :, 0:part], hid.at[e, :, part:2 * part], hsend.at[0, e], hrecv.at[0, e], {"tensor": sib})
+
+    def hid_across(e):
+        return remote(hid.at[e, :, 0:part], hid.at[e, :, 2 * part:3 * part], hsend.at[1, e], hrecv.at[1, e], {"tensor": across})
+
+    def hid_onward(e):
+        return remote(hid.at[e, :, 2 * part:3 * part], hid.at[e, :, 3 * part:4 * part], hsend.at[2, e], hrecv.at[2, e], {"tensor": sib})
+
+    def ret_copy(i, e):
+        to = lax.rem(z + i, n)
+        return remote(outs.at[e, to], back.at[z, e], rsend.at[i, e], rrecv.at[z, e], {"expert": to})
+
+    def second(i, carry):
+        @pl.when(i < local)
+        def _():
+            pre = acc[i] + partial(2, i) + partial(3, i)
+            gate, up = pre[:, :part], pre[:, part:]
+            hid[i, :, 0:part] = (gate / (1.0 + jnp.exp(-gate)) * up).astype(bf16)
+            hid_across(i).start()
+            hid_sib(i).start()
+
+        @pl.when((i >= lead) & (i < local + lead))
+        def _():
+            hid_across(i - lead).wait_recv()
+            hid_onward(i - lead).start()
+
+        @pl.when(i >= lag)
+        def _():
+            e = i - lag
+            hid_sib(e).wait_recv()
+            hid_onward(e).wait_recv()
+            got = jnp.dot(hid[e], wdb[e], preferred_element_type=f32).astype(bf16)
+            outs[e] = got.reshape(n, CAP, kd)
+            for step in range(1, n):
+                ret_copy(step, e).start()
+
+        return carry
+
+    lax.fori_loop(0, local + lag, second, 0)
+
+    sid0, sid1 = sids[z, 0:1, :], sids[z, 1:2, :]
+    g0, g1 = meta_ref[2:3, :], meta_ref[3:4, :]
+    for i in range(n):
+        frm = lax.rem(z + i, n)
+        if i == 0:
+            got = outs[:, z].reshape(slots, kd)
+        else:
+            for e in range(local):
+                remote(outs.at[e, z], back.at[frm, e], rsend.at[i, e], rrecv.at[frm, e], {"expert": frm}).wait_recv()
+            got = back[frm].reshape(slots, kd)
+        mine = (slot_names + frm * slots).astype(f32)
+        spread = (jnp.where(mine == sid0, g0, 0.0) + jnp.where(mine == sid1, g1, 0.0)).T
+        high = spread.astype(bf16)
+        low = (spread - high.astype(f32)).astype(bf16)
+        term = jnp.dot(high, got, preferred_element_type=f32) + jnp.dot(low, got, preferred_element_type=f32)
+        out_ref[...] = term if i == 0 else out_ref[...] + term
+
+    each_way(lambda d: tok_copy(d, z, True).wait_send())
+    each_way(lambda d: sid_copy(d, z).wait_send())
+
+    def left(src, d):
+        @pl.when(can_forward(d))
+        def _():
+            tok_copy(d, src, False).wait_send()
+            sid_copy(d, src).wait_send()
+
+    for k in range(1, n):
+        at_step(k, left)
+    for s in range(n):
+        sib_copy(s).wait_send()
+        across_copy(s).wait_send()
+        onward_copy(s).wait_send()
+    for e in range(local):
+        hid_sib(e).wait_send()
+        hid_across(e).wait_send()
+        hid_onward(e).wait_send()
+        for step in range(1, n):
+            ret_copy(step, e).wait_send()
+
+
+def fused_device(
+    n, tokens, expert_ids, gate_values, teacher_out, student_gate, student_up, student_down
+):
+    rows, kd = tokens.shape
+    slabs, half, full = student_gate.shape
+    local, part = slabs // 2, 2 * half
+    meta = jnp.concatenate(
+        [expert_ids.T.astype(jnp.float32), gate_values.T, jnp.zeros((4, rows), jnp.float32)], axis=0
+    )
+    wg = student_gate.reshape(local, part, full)
+    wu = student_up.reshape(local, part, full)
+    wd = student_down.reshape(local, 2, student_down.shape[1], kd)
+    bf16, f32 = jnp.bfloat16, jnp.float32
+    dma = pltpu.SemaphoreType.DMA
+    vmem = pl.BlockSpec(memory_space=pltpu.VMEM)
+    hbm = pl.BlockSpec(memory_space=pl.ANY)
+    student = pl.pallas_call(
+        functools.partial(fused_kernel, n, 2, 4),
+        out_shape=jax.ShapeDtypeStruct((rows, kd), f32),
+        in_specs=[vmem, vmem, hbm, hbm, hbm],
+        out_specs=vmem,
+        scratch_shapes=[
+            pltpu.VMEM((4, local, 2 * part, kd), bf16),
+            pltpu.VMEM((local, 4 * part, kd), bf16),
+            pltpu.VMEM((n, rows, kd), bf16),
+            pltpu.VMEM((n, 8, rows), f32),
+            pltpu.VMEM((4, n, local, CAP, kd), bf16),
+            pltpu.VMEM((local, n * CAP, 2 * part), f32),
+            pltpu.VMEM((local, n * CAP, 4 * part), bf16),
+            pltpu.VMEM((local, n, CAP, kd), bf16),
+            pltpu.VMEM((n, local, CAP, kd), bf16),
+            dma((4, 2)), dma((4, 2)), dma((2, n)), dma((n,)), dma((2, n)), dma((n,)),
+            dma((n,)), dma((n,)), dma((n,)), dma((n,)), dma((n,)), dma((n,)),
+            dma((3, local)), dma((3, local)), dma((n, local)), dma((n, local)),
+        ],
+        compiler_params=pltpu.CompilerParams(
+            collective_id=0, has_side_effects=True, vmem_limit_bytes=63 * 1024 * 1024
+        ),
+        cost_estimate=pl.CostEstimate(
+            flops=6 * local * n * CAP * 2 * part * full, bytes_accessed=6 * slabs * half * full,
+            transcendentals=0,
+        ),
+    )(meta, tokens, wg, wu, wd)
+    return (student, teacher_out - student)
+
+
 def solution(mesh):
     in_specs = (
         P(("groups", "expert"), "tensor"),
@@ -79,6 +381,9 @@
         P("expert", None, "tensor"),
     )
     out_specs = (P(("groups", "expert"), "tensor"), P(("groups", "expert"), "tensor"))
+    sizes = dict(mesh.shape)
+    fused = sizes["tensor"] == 4 and 2 * sizes["expert"] <= EXPERTS // 2 and sizes["expert"] == 4
+    body = functools.partial(fused_device, sizes["expert"]) if fused else per_device
     return jax.shard_map(
-        per_device, mesh=mesh, in_specs=in_specs, out_specs=out_specs, check_vma=False
-    )
+        body, mesh=mesh, in_specs=in_specs, out_specs=out_specs, check_vma=False
+    )

time: 280 us -> 74 us (0.26)
  blocking collectives: 152 us -> 0 us
  waiting for transfers between devices: 74.7 us -> 0 us
  Pallas kernels: 0 us -> 67.2 us
  matrix products: 33.5 us -> 0 us
  between operations: 14.2 us -> 0.66 us
    all_to_all x2 -> x0, blocking collectives: 152 us -> none  [the longest x1 98.1 us: per_device(): lax.all_to_all(flat_out, 'expert', split_axis=0, concat_axis=0, tiled=True)]
    all_gather x2 -> x0, waiting for transfers between devices: 74.6 us -> none  [the longest x1 57.6 us: per_device(): lax.all_gather(lax.all_to_all(doubled.reshape(2 * EXPERTS, CAP, width), '...]
    pallas_call x0 -> x1, Pallas kernels: none -> 67.2 us  [fused_device(): pl.pallas_call(functools.partial(fused_kernel, n, 2, 4), out_shape=jax.Sh...]
    dot_general x5 -> x0, matrix products: 33.5 us -> none  [the longest x1 11.4 us: per_device(): jnp.einsum('nsid,shd->nsih', grouped, student_gate, preferred_element_typ...]
  transfers between devices with their start and end apart: 2 -> 0, of which waited for: 2 -> 0; matrix products, arithmetic and copies ran while one was open for 0% -> 0% of each run, Pallas kernels for 0% -> 0%
where the time goes in v1:
time: 74 us; the launch traced here: 73.7 us
  Pallas kernels  67.2 us (91%)
  other arithmetic  3.92 us (5%)
  local copies, waits for them, and re-layouts  1.96 us (3%)
    pallas_call x1, Pallas kernels, fused_device(): pl.pallas_call(functools.partial(fused_kernel, n, 2, 4), out_shape=jax.Sh...  67.2 us
    sub x1, other arithmetic, fused_device(): return (student, teacher_out - student)  1.9 us
    unnamed x3, local copies, waits for them, and re-layouts  1.89 us

profile of v1, /device:TPU:0, one launch (start us, length us, event | category | flops | bytes accessed | tf_op | source)
XLA Modules:
  0.0 73.7 jit_solution(1663395309210972180)
XLA Ops:
  0.6 0.1 pad.2.clone
  0.7 0.7 convert_bitcast_fusion
  1.4 1.3 %maximum_maximum_fusion.meta_ref = f32[8,128]{1,0:T(8,128)} fusion(f32[2,128]{1,0:T(2,128)} %bitcast.9, f32[2,128]{1,0:T(2,128)S(1)} %convert_bitcast_fusion, f32[8]{0:T(128)S(1)} %pad.2.clone), kind=kLoop, calls=%fused_computation | loop fusion | flops 2048 | bytes 6176 | tf_op jit(solution)/shard_map/concatenate | solution.py:333
  2.7 0.0 copy-start
  2.7 67.2 %shard_map.86 = f32[128,1024]{1,0:T(8,128)} custom-call(f32[8,128]{1,0:T(8,128)} %maximum_maximum_fusion.meta_ref, bf16[128,1024]{1,0:T(8,128)(2,1)} %tok_ref.1, bf16[8,256,4096]{2,1,0:T(8,128)(2,1)} %bitcast.6, bf16[8,256,4096]{2,1,0:T(8,128)(2,1)} %bitcast.7, bf16[8,2,512,1024]{3,2,1,0:T(8,128)(2,1)} %bitcast.8), custom_call_target="tpu_custom_call" | custom-call | flops 6442450944 | bytes 50331648 | tf_op jit(solution)/shard_map/pallas_call | solution.py:343
  69.9 0.0 copy-done
  69.9 1.9 %sub.3 = f32[128,1024]{1,0:T(8,128)} subtract(f32[128,1024]{1,0:T(8,128)S(1)} %copy-done, f32[128,1024]{1,0:T(8,128)} %shard_map.86) | non-fusion elementwise | flops 131072 | bytes 1572864 | tf_op jit(solution)/shard_map/sub | solution.py:370
  71.8 1.9 %copy.10 = f32[128,1024]{1,0:T(8,128)} copy(f32[128,1024]{1,0:T(8,128)} %shard_map.86) | data formatting | bytes 1048576
  (1 shorter events, 0.0 us)
Async XLA Ops:
  2.7 67.2 %copy-start = (f32[128,1024]{1,0:T(8,128)S(1)}, f32[128,1024]{1,0:T(8,128)}, u32[]{:S(2)}) copy-start(f32[128,1024]{1,0:T(8,128)} %param.10) | copy-start | bytes 1572868

commit v2 on v1

--- a/solution.py
+++ b/solution.py
@@ -72,7 +72,7 @@
 
 
 def fused_kernel(
-    n, lead, lag, meta_ref, tok_ref, wg_ref, wu_ref, wd_ref, out_ref,
+    n, lead, lag, ids_ref, gates_ref, tok_ref, wg_ref, wu_ref, wd_ref, out_ref,
     wgu, wdb, gath, sids, packed, acc, hid, outs, back,
     wsem, dsem, zsend, zrecv, msend, mrecv, ssend, srecv, xsend, xrecv, fsend, frecv,
     hsend, hrecv, rsend, rrecv,
@@ -85,6 +85,7 @@
     local, part = wg_ref.shape[0], wg_ref.shape[1]
     half = part // 2
     slots = local * CAP
+    parts, cd = gath.shape[1], gath.shape[3]
     f32, bf16 = jnp.float32, jnp.bfloat16
 
     def remote(src, dst, send, recv, where):
@@ -122,9 +123,9 @@
         pl.semaphore_signal(barrier, inc=1, device_id=peer, device_id_type=pl.DeviceIdType.MESH)
     pl.semaphore_wait(barrier, len(peers))
 
-    def tok_copy(d, src, own):
-        ref = tok_ref if own else gath.at[src]
-        return remote(ref, gath.at[src], zsend.at[d, src], zrecv.at[src], {"expert": z + 1 - 2 * d})
+    def tok_copy(d, c, src, own):
+        ref = tok_ref.at[:, c * cd:(c + 1) * cd] if own else gath.at[src, c]
+        return remote(ref, gath.at[src, c], zsend.at[d, c, src], zrecv.at[c, src], {"expert": z + 1 - 2 * d})
 
     def sid_copy(d, src):
         return remote(sids.at[src], sids.at[src], msend.at[d, src], mrecv.at[src], {"expert": z + 1 - 2 * d})
@@ -138,9 +139,9 @@
         def _():
             fn(1)
 
-    each_way(lambda d: tok_copy(d, z, True).start())
-
-    id0, id1 = meta_ref[0:1, :], meta_ref[1:2, :]
+    each_way(lambda d: tok_copy(d, 0, z, True).start())
+
+    id0, id1 = ids_ref[0:1, :].astype(f32), ids_ref[1:2, :].astype(f32)
     names = lax.broadcasted_iota(jnp.int32, (n * local, rows), 0).astype(f32)
     hit0, hit1 = names == id0, names == id1
     hits = (jnp.where(hit0, 1.0, 0.0) + jnp.where(hit1, 1.0, 0.0)).astype(bf16)
@@ -157,91 +158,112 @@
 
     slot_names = lax.broadcasted_iota(jnp.int32, (slots, rows), 0)
 
-    def sib_copy(src):
-        return remote(packed.at[0, src], packed.at[1, src], ssend.at[src], srecv.at[src], {"tensor": sib})
-
-    def across_copy(src):
-        return remote(packed.at[0, src], packed.at[2, src], xsend.at[src], xrecv.at[src], {"tensor": across})
-
-    def onward_copy(src):
-        return remote(packed.at[2, src], packed.at[3, src], fsend.at[src], frecv.at[src], {"tensor": sib})
-
-    def pick(src, own):
+    def sib_copy(c, src):
+        return remote(packed.at[0, c, src], packed.at[1, c, src], ssend.at[c, src], srecv.at[c, src], {"tensor": sib})
+
+    def across_copy(c, src):
+        return remote(packed.at[0, c, src], packed.at[2, c, src], xsend.at[c, src], xrecv.at[c, src], {"tensor": across})
+
+    def onward_copy(c, src):
+        return remote(packed.at[2, c, src], packed.at[3, c, src], fsend.at[c, src], frecv.at[c, src], {"tensor": sib})
+
+    def pick(c, src, own):
         mine = (slot_names + z * slots).astype(f32)
         a, b = sids[src, 0:1, :], sids[src, 1:2, :]
         picker = (jnp.where(mine == a, 1.0, 0.0) + jnp.where(mine == b, 1.0, 0.0)).astype(bf16)
-        toks = tok_ref[...] if own else gath[src]
+        toks = tok_ref[:, c * cd:(c + 1) * cd] if own else gath[src, c]
         got = jnp.dot(picker, toks, preferred_element_type=f32).astype(bf16)
-        packed[0, src] = got.reshape(local, CAP, kd)
-        across_copy(src).start()
-        sib_copy(src).start()
-
-    def at_step(k, fn):
+        packed[0, c, src] = got.reshape(local, CAP, cd)
+        across_copy(c, src).start()
+        sib_copy(c, src).start()
+
+    def at_step(k, fn, c):
         if k == 0:
-            fn(z, None)
+            fn(c, z, None)
             return
 
         @pl.when(z >= k)
         def _():
-            fn(z - k, 0)
+            fn(c, z - k, 0)
 
         @pl.when(z + k < n)
         def _():
-            fn(z + k, 1)
+            fn(c, z + k, 1)
 
     def can_forward(d):
         return z < n - 1 if d == 0 else z > 0
 
-    def arrive(src, d):
-        tok_copy(d, src, False).wait_recv()
-        sid_copy(d, src).wait_recv()
+    def arrive(c, src, d):
+        tok_copy(d, c, src, False).wait_recv()
+        if c == 0:
+            sid_copy(d, src).wait_recv()
 
         @pl.when(can_forward(d))
         def _():
-            tok_copy(d, src, False).start()
-            sid_copy(d, src).start()
-
-        pick(src, False)
-
-    def onward(src, d):
-        across_copy(src).wait_recv()
-        onward_copy(src).start()
-
-    pick(z, True)
+            tok_copy(d, c, src, False).start()
+            if c == 0:
+                sid_copy(d, src).start()
+
+        pick(c, src, False)
+
+    def onward(c, src, d):
+        across_copy(c, src).wait_recv()
+        onward_copy(c, src).start()
+
+    nt = (((1,), (1,)), ((), ()))
+
+    def partial(c, e):
+        total = None
+        for j in range(4):
+            term = lax.dot_general(
+                packed[j, c, :, e].reshape(n * CAP, cd), wgu[j, e, :, c * cd:(c + 1) * cd],
+                nt, preferred_element_type=f32,
+            )
+            total = term if total is None else total + term
+        return total
+
+    def settle(c):
+        for s in range(n):
+            sib_copy(c, s).wait_recv()
+            onward_copy(c, s).wait_recv()
+
+    def early(c):
+        def run(e, carry):
+            acc[e] = partial(c, e) if c == 0 else acc[e] + partial(c, e)
+            return carry
+
+        lax.fori_loop(0, local, run, 0)
+
+    pick(0, z, True)
     for k in range(1, n):
-        at_step(k, arrive)
+        at_step(k, arrive, 0)
+        if k == 1:
+            for c in range(1, parts):
+                each_way(lambda d: tok_copy(d, c, z, True).start())
+                pick(c, z, True)
         if k >= 2:
-            at_step(k - 2, onward)
-
-    nt = (((1,), (1,)), ((), ()))
-
-    def rows_of(j, e):
-        return packed[j, :, e].reshape(n * CAP, kd)
-
-    def partial(j, e):
-        return lax.dot_general(rows_of(j, e), wgu[j, e], nt, preferred_element_type=f32)
-
-    for s in range(n):
-        sib_copy(s).wait_recv()
-    for j in range(2):
-        for c in weight_copies[j]:
-            c.wait()
-
-    def first(e, carry):
-        acc[e] = partial(0, e) + partial(1, e)
-        return carry
-
-    lax.fori_loop(0, local, first, 0)
-
-    for k in range(max(n - 2, 0), n):
-        at_step(k, onward)
-    for s in range(n):
-        onward_copy(s).wait_recv()
-    for j in range(2, 4):
-        for c in weight_copies[j]:
-            c.wait()
-    for c in down_copies:
-        c.wait()
+            at_step(k - 2, onward, 0)
+    behind = [(0, n - 2), (0, n - 1)]
+    for c in range(1, parts):
+        behind.append((c, 0))
+        for k in range(1, n):
+            at_step(k, arrive, c)
+            at_step(behind[0][1], onward, behind[0][0])
+            behind = behind[1:] + [(c, k)]
+    for pair in weight_copies:
+        for w in pair:
+            w.wait()
+    for c in range(parts - 1):
+        while behind and behind[0][0] == c:
+            at_step(behind[0][1], onward, c)
+            behind = behind[1:]
+        settle(c)
+        early(c)
+    for c, k in behind:
+        at_step(k, onward, c)
+    settle(parts - 1)
+    for w in down_copies:
+        w.wait()
 
     def hid_sib(e):
         return remote(hid.at[e, :, 0:part], hid.at[e, :, part:2 * part], hsend.at[0, e], hrecv.at[0, e], {"tensor": sib})
@@ -259,7 +281,7 @@
     def second(i, carry):
         @pl.when(i < local)
         def _():
-            pre = acc[i] + partial(2, i) + partial(3, i)
+            pre = acc[i] + partial(parts - 1, i)
             gate, up = pre[:, :part], pre[:, part:]
             hid[i, :, 0:part] = (gate / (1.0 + jnp.exp(-gate)) * up).astype(bf16)
             hid_across(i).start()
@@ -277,6 +299,7 @@
             hid_onward(e).wait_recv()
             got = jnp.dot(hid[e], wdb[e], preferred_element_type=f32).astype(bf16)
             outs[e] = got.reshape(n, CAP, kd)
+            back[z, e] = outs[e, z]
             for step in range(1, n):
                 ret_copy(step, e).start()
 
@@ -285,37 +308,41 @@
     lax.fori_loop(0, local + lag, second, 0)
 
     sid0, sid1 = sids[z, 0:1, :], sids[z, 1:2, :]
-    g0, g1 = meta_ref[2:3, :], meta_ref[3:4, :]
-    for i in range(n):
-        frm = lax.rem(z + i, n)
-        if i == 0:
-            got = outs[:, z].reshape(slots, kd)
-        else:
-            for e in range(local):
+    g0, g1 = gates_ref[0:1, :], gates_ref[1:2, :]
+    cuts = (0, max(local - 2, 1), local)
+    for lo, hi in zip(cuts[:-1], cuts[1:]):
+        for i in range(1, n):
+            frm = lax.rem(z + i, n)
+            for e in range(lo, hi):
                 remote(outs.at[e, z], back.at[frm, e], rsend.at[i, e], rrecv.at[frm, e], {"expert": frm}).wait_recv()
-            got = back[frm].reshape(slots, kd)
-        mine = (slot_names + frm * slots).astype(f32)
+        size = (hi - lo) * CAP
+        got = back[:, lo:hi].reshape(n * size, kd)
+        ramp = lax.broadcasted_iota(jnp.int32, (size, rows), 0)
+        mine = jnp.concatenate([ramp + (s * slots + lo * CAP) for s in range(n)], axis=0).astype(f32)
         spread = (jnp.where(mine == sid0, g0, 0.0) + jnp.where(mine == sid1, g1, 0.0)).T
         high = spread.astype(bf16)
         low = (spread - high.astype(f32)).astype(bf16)
         term = jnp.dot(high, got, preferred_element_type=f32) + jnp.dot(low, got, preferred_element_type=f32)
-        out_ref[...] = term if i == 0 else out_ref[...] + term
-
-    each_way(lambda d: tok_copy(d, z, True).wait_send())
+        out_ref[...] = term if lo == 0 else out_ref[...] + term
+
+    for c in range(parts):
+        each_way(lambda d: tok_copy(d, c, z, True).wait_send())
     each_way(lambda d: sid_copy(d, z).wait_send())
 
-    def left(src, d):
+    def left(c, src, d):
         @pl.when(can_forward(d))
         def _():
-            tok_copy(d, src, False).wait_send()
-            sid_copy(d, src).wait_send()
-
-    for k in range(1, n):
-        at_step(k, left)
-    for s in range(n):
-        sib_copy(s).wait_send()
-        across_copy(s).wait_send()
-        onward_copy(s).wait_send()
+            tok_copy(d, c, src, False).wait_send()
+            if c == 0:
+                sid_copy(d, src).wait_send()
+
+    for c in range(parts):
+        for k in range(1, n):
+            at_step(k, left, c)
+        for s in range(n):
+            sib_copy(c, s).wait_send()
+            across_copy(c, s).wait_send()
+            onward_copy(c, s).wait_send()
     for e in range(local):
         hid_sib(e).wait_send()
         hid_across(e).wait_send()
@@ -324,15 +351,18 @@
             ret_copy(step, e).wait_send()
 
 
+def finish_kernel(student_ref, teacher_ref, out_ref, residual_ref):
+    out_ref[...] = student_ref[...]
+    residual_ref[...] = teacher_ref[...] - student_ref[...]
+
+
 def fused_device(
     n, tokens, expert_ids, gate_values, teacher_out, student_gate, student_up, student_down
 ):
     rows, kd = tokens.shape
     slabs, half, full = student_gate.shape
     local, part = slabs // 2, 2 * half
-    meta = jnp.concatenate(
-        [expert_ids.T.astype(jnp.float32), gate_values.T, jnp.zeros((4, rows), jnp.float32)], axis=0
-    )
+    parts = 2
     wg = student_gate.reshape(local, part, full)
     wu = student_up.reshape(local, part, full)
     wd = student_down.reshape(local, 2, student_down.shape[1], kd)
@@ -343,20 +373,20 @@
     student = pl.pallas_call(
         functools.partial(fused_kernel, n, 2, 4),
         out_shape=jax.ShapeDtypeStruct((rows, kd), f32),
-        in_specs=[vmem, vmem, hbm, hbm, hbm],
+        in_specs=[vmem, vmem, vmem, hbm, hbm, hbm],
         out_specs=vmem,
         scratch_shapes=[
             pltpu.VMEM((4, local, 2 * part, kd), bf16),
             pltpu.VMEM((local, 4 * part, kd), bf16),
-            pltpu.VMEM((n, rows, kd), bf16),
+            pltpu.VMEM((n, parts, rows, kd // parts), bf16),
             pltpu.VMEM((n, 8, rows), f32),
-            pltpu.VMEM((4, n, local, CAP, kd), bf16),
+            pltpu.VMEM((4, parts, n, local, CAP, kd // parts), bf16),
             pltpu.VMEM((local, n * CAP, 2 * part), f32),
             pltpu.VMEM((local, n * CAP, 4 * part), bf16),
             pltpu.VMEM((local, n, CAP, kd), bf16),
             pltpu.VMEM((n, local, CAP, kd), bf16),
-            dma((4, 2)), dma((4, 2)), dma((2, n)), dma((n,)), dma((2, n)), dma((n,)),
-            dma((n,)), dma((n,)), dma((n,)), dma((n,)), dma((n,)), dma((n,)),
+            dma((4, 2)), dma((4, 2)), dma((2, parts, n)), dma((parts, n)), dma((2, n)), dma((n,)),
+            dma((parts, n)), dma((parts, n)), dma((parts, n)), dma((parts, n)), dma((parts, n)), dma((parts, n)),
             dma((3, local)), dma((3, local)), dma((n, local)), dma((n, local)),
         ],
         compiler_params=pltpu.CompilerParams(
@@ -366,8 +396,15 @@
             flops=6 * local * n * CAP * 2 * part * full, bytes_accessed=6 * slabs * half * full,
             transcendentals=0,
         ),
-    )(meta, tokens, wg, wu, wd)
-    return (student, teacher_out - student)
+    )(expert_ids.T, gate_values.T, tokens, wg, wu, wd)
+    block = pl.BlockSpec((rows // 2, kd), lambda i: (i, 0))
+    return tuple(pl.pallas_call(
+        finish_kernel,
+        grid=(2,),
+        out_shape=[jax.ShapeDtypeStruct((rows, kd), f32)] * 2,
+        in_specs=[block, block],
+        out_specs=[block, block],
+    )(student, teacher_out))
 
 
 def solution(mesh):

time: 74 us -> 69 us (0.932)
  other arithmetic: 3.92 us -> 0 us
  local copies, waits for them, and re-layouts: 1.96 us -> 0 us
  Pallas kernels: 67.2 us -> 68.2 us
    pallas_call x0 -> x1, Pallas kernels: none -> 2.04 us  [fused_device(): pl.pallas_call(finish_kernel, grid=(2,), out_shape=[jax.ShapeDtypeStruct(...]
    sub x1 -> x0, other arithmetic: 1.9 us -> none  [fused_device(): return (student, teacher_out - student)]
    unnamed x3 -> x0, local copies, waits for them, and re-layouts: 1.89 us -> none
    concatenate x1 -> x0, other arithmetic: 1.34 us -> none  [fused_device(): jnp.concatenate([expert_ids.T.astype(jnp.float32), gate_values.T, jnp.zer...]
    pallas_call x1, Pallas kernels: 67.2 us -> 66.2 us  [fused_device(): pl.pallas_call(functools.partial(fused_kernel, n, 2, 4), out_shape=jax.Sh...]
where the time goes in v2:
time: 69 us; the launch traced here: 68.8 us
  Pallas kernels  68.2 us (99%)
    pallas_call x1, Pallas kernels, fused_device(): pl.pallas_call(functools.partial(fused_kernel, n, 2, 4), out_shape=jax.Sh...  66.2 us
    pallas_call x1, Pallas kernels, fused_device(): pl.pallas_call(finish_kernel, grid=(2,), out_shape=[jax.ShapeDtypeStruct(...  2.04 us

profile of v2, /device:TPU:0, one launch (start us, length us, event | category | flops | bytes accessed | tf_op | source)
XLA Modules:
  0.0 68.8 jit_solution(15930227434112952860)
XLA Ops:
  0.6 66.2 %shard_map.86.student_ref = f32[128,1024]{1,0:T(8,128)} custom-call(s32[2,128]{1,0:T(2,128)} %bitcast.8, f32[2,128]{1,0:T(2,128)} %bitcast.9, bf16[128,1024]{1,0:T(8,128)(2,1)} %tok_ref.1, bf16[8,256,4096]{2,1,0:T(8,128)(2,1)} %bitcast.5, bf16[8,256,4096]{2,1,0:T(8,128)(2,1)} %bitcast.6, bf16[8,2,512,1024]{3,2,1,0:T(8,128)(2,1)} %bitcast.7), custom_call_target="tpu_custom_call" | custom-call | flops 6442450944 | bytes 50331648 | tf_op jit(solution)/shard_map/pallas_call | solution.py:373
  66.8 2.0 %shard_map.87 = (f32[128,1024]{1,0:T(8,128)}, f32[128,1024]{1,0:T(8,128)}) custom-call(f32[128,1024]{1,0:T(8,128)} %shard_map.86.student_ref, f32[128,1024]{1,0:T(8,128)} %teacher_ref.1), custom_call_target="tpu_custom_call" | custom-call | tf_op jit(solution)/shard_map/pallas_call | solution.py:401

commit v3 on v2

--- a/solution.py
+++ b/solution.py
@@ -235,12 +235,11 @@
         lax.fori_loop(0, local, run, 0)
 
     pick(0, z, True)
+    for c in range(1, parts):
+        each_way(lambda d: tok_copy(d, c, z, True).start())
+        pick(c, z, True)
     for k in range(1, n):
         at_step(k, arrive, 0)
-        if k == 1:
-            for c in range(1, parts):
-                each_way(lambda d: tok_copy(d, c, z, True).start())
-                pick(c, z, True)
         if k >= 2:
             at_step(k - 2, onward, 0)
     behind = [(0, n - 2), (0, n - 1)]

time: 69 us -> 68.2 us (0.988)
  Pallas kernels: 68.2 us -> 67.4 us
    pallas_call x1, Pallas kernels: 66.2 us -> 65.3 us  [fused_device(): pl.pallas_call(functools.partial(fused_kernel, n, 2, 4), out_shape=jax.Sh...]
where the time goes in v3:
time: 68.2 us; the launch traced here: 68 us
  Pallas kernels  67.4 us (99%)
    pallas_call x1, Pallas kernels, fused_device(): pl.pallas_call(functools.partial(fused_kernel, n, 2, 4), out_shape=jax.Sh...  65.3 us
    pallas_call x1, Pallas kernels, fused_device(): pl.pallas_call(finish_kernel, grid=(2,), out_shape=[jax.ShapeDtypeStruct(...  2.04 us

profile of v3, /device:TPU:0, one launch (start us, length us, event | category | flops | bytes accessed | tf_op | source)
XLA Modules:
  0.0 68.0 jit_solution(34275566037726856)
XLA Ops:
  0.6 65.3 %shard_map.86.student_ref = f32[128,1024]{1,0:T(8,128)} custom-call(s32[2,128]{1,0:T(2,128)} %bitcast.8, f32[2,128]{1,0:T(2,128)} %bitcast.9, bf16[128,1024]{1,0:T(8,128)(2,1)} %tok_ref.1, bf16[8,256,4096]{2,1,0:T(8,128)(2,1)} %bitcast.5, bf16[8,256,4096]{2,1,0:T(8,128)(2,1)} %bitcast.6, bf16[8,2,512,1024]{3,2,1,0:T(8,128)(2,1)} %bitcast.7), custom_call_target="tpu_custom_call" | custom-call | flops 6442450944 | bytes 50331648 | tf_op jit(solution)/shard_map/pallas_call | solution.py:372
  66.0 2.0 %shard_map.87 = (f32[128,1024]{1,0:T(8,128)}, f32[128,1024]{1,0:T(8,128)}) custom-call(f32[128,1024]{1,0:T(8,128)} %shard_map.86.student_ref, f32[128,1024]{1,0:T(8,128)} %teacher_ref.1), custom_call_target="tpu_custom_call" | custom-call | tf_op jit(solution)/shard_map/pallas_call | solution.py:400
